TPU v7x, 32 devices: a whole 2x2x4 slice. The times are simulated.
32 devices in a mesh: tok: 8 (over z, x), head: 4 (over y, core).
Axes of the slice: x: 2, y: 2, z: 4, core: 2. Of those that a mesh axis runs over, the one named last changes fastest.
Arguments:
- hidden: bfloat16 [1024, 2048], P('tok'), may hold values from -6 to 6
- norm_gain: float32 [2048], replicated, may hold values from 0.1 to 1.9
- w_router: bfloat16 [2048, 8], replicated, may hold values from -0.125 to 0.125
- w_query: bfloat16 [8, 2048, 2048], P(None, None, 'head'), may hold values from -0.125 to 0.125
- w_key: bfloat16 [2048, 2048], P(None, 'head'), may hold values from -0.125 to 0.125
- w_value: bfloat16 [2048, 2048], P(None, 'head'), may hold values from -0.125 to 0.125
- w_out: bfloat16 [8, 2048, 2048], P(None, 'head'), may hold values from -0.125 to 0.125
- key_pool: bfloat16 [64, 128, 2048], P('tok', None, 'head'), may hold values from -48 to 48
- value_pool: bfloat16 [64, 128, 2048], P('tok', None, 'head'), may hold values from -6 to 6
- page_table: int32 [4, 16], replicated, may hold values from 0 to 63, as said below
- request_group: int32 [8], replicated, may hold values from 0 to 3, as said below
- suffix_len: int32 [8], P('tok'), may hold values from 1 to 128, as said below
- att_experts: int32 [1024, 2], P('tok'), may hold values from 0 to 7, all different within a row
Outputs:
- attended: bfloat16 [1024, 2048], P('tok', 'head')
Inputs may be any that keep to these rules, and one draw needn't show every extreme that they name: `page_table`: each of the 64 pool pages appears exactly once in the table. `request_group`: each prefix is shared by exactly 2 requests. `suffix_len`: some request has all 128 slots live.
All inputs are finite; a program needn't handle non-finite values.
Results may differ from a plain program's by a relative error of at most 0.015.
Values may be sent and summed in bfloat16 or wider, within the bound.
A program may use at most 128 MiB of HBM per device.

v0:
```python
import jax
import jax.numpy as jnp
from jax import lax
from jax.sharding import PartitionSpec as P

HD = 128


def rotate(values, positions):
    half = values.shape[-1] // 2
    freq = 10000.0 ** (-jnp.arange(half, dtype=jnp.float32) * 2.0 / values.shape[-1])
    angle = positions.astype(jnp.float32)[:, None] * freq[None, :]
    shape = (values.shape[0],) + (1,) * (values.ndim - 2) + (half,)
    cosine = jnp.cos(angle).reshape(shape)
    sine = jnp.sin(angle).reshape(shape)
    first = values[..., :half]
    second = values[..., half:]
    return jnp.concatenate(
        [first * cosine - second * sine, second * cosine + first * sine], axis=-1
    )


def partial_attention(query, keys, values, mask):
    scale = 1.0 / keys.shape[-1] ** 0.5
    scores = jnp.einsum("rshd,khd->rshk", query, keys, preferred_element_type=jnp.float32) * scale
    if mask is not None:
        scores = jnp.where(mask[:, None, None, :], scores, -1e30)
    top = jnp.max(scores, axis=-1)
    weights = jnp.exp(scores - top[..., None])
    total = jnp.sum(weights, axis=-1)
    out = jnp.einsum(
        "rshk,khd->rshd", weights.astype(jnp.bfloat16), values, preferred_element_type=jnp.float32
    )
    return (top, total, out)


def combine(first, second):
    top = jnp.maximum(first[0], second[0])
    scale_a = jnp.exp(first[0] - top)
    scale_b = jnp.exp(second[0] - top)
    total = first[1] * scale_a + second[1] * scale_b
    out = first[2] * scale_a[..., None] + second[2] * scale_b[..., None]
    return (top, total, out)


def per_device(
    hidden,
    norm_gain,
    w_router,
    w_query,
    w_key,
    w_value,
    w_out,
    key_pool,
    value_pool,
    page_table,
    request_group,
    suffix_len,
    att_experts,
):
    tok_dev = hidden.shape[0]
    req_dev = suffix_len.shape[0]
    suffix = tok_dev // req_dev
    local_cols = w_key.shape[1]
    local_heads = local_cols // HD
    experts = w_query.shape[0]
    topk = att_experts.shape[1]
    page_rows = key_pool.shape[1]
    prefix_len = page_table.shape[1] * page_rows
    state = hidden.astype(jnp.float32)
    normed = (
        state * lax.rsqrt(jnp.mean(state * state, axis=-1, keepdims=True) + 1e-06) * norm_gain
    ).astype(jnp.bfloat16)
    logits = jnp.dot(normed, w_router, preferred_element_type=jnp.float32)
    gates = jax.nn.softmax(jnp.take_along_axis(logits, att_experts, axis=1), axis=-1)
    positions = jnp.arange(tok_dev, dtype=jnp.int32) % suffix + prefix_len
    every_expert = jnp.einsum("td,edc->tec", normed, w_query, preferred_element_type=jnp.float32)
    chosen = att_experts[:, :, None] == jnp.arange(experts, dtype=jnp.int32)[None, None, :]
    selected = jnp.einsum(
        "tse,tec->tsc", chosen.astype(jnp.float32), every_expert, precision=lax.Precision.HIGHEST
    )
    query = rotate(selected.reshape(tok_dev, topk, local_heads, HD), positions).astype(jnp.bfloat16)
    keys = rotate(
        jnp.dot(normed, w_key, preferred_element_type=jnp.float32).reshape(
            tok_dev, local_heads, HD
        ),
        positions,
    ).astype(jnp.bfloat16)
    vals = (
        jnp.dot(normed, w_value, preferred_element_type=jnp.float32)
        .astype(jnp.bfloat16)
        .reshape(tok_dev, local_heads, HD)
    )
    query_req = query.reshape(req_dev, suffix, topk, local_heads, HD)
    rows = jnp.arange(suffix, dtype=jnp.int32)

    def suffix_part(q_rows, k_rows, v_rows, length):
        mask = (rows[None, :] <= rows[:, None]) & (rows[None, :] < length)
        return partial_attention(q_rows, k_rows, v_rows, mask)

    second = jax.vmap(suffix_part)(
        query_req,
        keys.reshape(req_dev, suffix, local_heads, HD),
        vals.reshape(req_dev, suffix, local_heads, HD),
        suffix_len,
    )
    all_keys, all_vals = (
        lax.all_gather(key_pool, "tok", axis=0, tiled=True),
        lax.all_gather(value_pool, "tok", axis=0, tiled=True),
    )
    base = lax.axis_index("tok") * req_dev
    groups_here = lax.dynamic_slice_in_dim(request_group, base, req_dev)
    blocks = suffix // suffix

    def one_request(items):
        q_rows, group = items
        pages = page_table[group]
        prefix_keys = jnp.take(all_keys, pages, axis=0).reshape(prefix_len, local_heads, HD)
        prefix_vals = jnp.take(all_vals, pages, axis=0).reshape(prefix_len, local_heads, HD)

        def one_block(q_block):
            return partial_attention(q_block, prefix_keys, prefix_vals, None)

        b_top, b_total, b_out = lax.map(
            one_block, q_rows.reshape(blocks, suffix, topk, local_heads, HD)
        )
        return (
            b_top.reshape(suffix, topk, local_heads),
            b_total.reshape(suffix, topk, local_heads),
            b_out.reshape(suffix, topk, local_heads, HD),
        )

    first = lax.map(one_request, (query_req, groups_here))
    top, total, out = combine(first, second)
    valid = (rows[None, :] < suffix_len[:, None]).astype(jnp.float32)
    attention = (out / total[..., None] * valid[:, :, None, None, None]).reshape(
        tok_dev, topk, local_cols
    )
    weighted = (gates[:, :, None] * attention).astype(jnp.bfloat16)
    picked = jnp.sum(
        jnp.where(chosen[:, :, :, None], weighted[:, :, None, :], jnp.zeros((), jnp.bfloat16)),
        axis=1,
    )
    partial_out = jnp.einsum("tec,ecd->td", picked, w_out, preferred_element_type=jnp.float32)
    return lax.psum_scatter(
        partial_out.astype(jnp.bfloat16), "head", scatter_dimension=1, tiled=True
    )


def solution(mesh):
    return jax.shard_map(
        per_device,
        mesh=mesh,
        in_specs=(
            P("tok", None),
            P(),
            P(),
            P(None, None, "head"),
            P(None, "head"),
            P(None, "head"),
            P(None, "head", None),
            P("tok", None, "head"),
            P("tok", None, "head"),
            P(),
            P(),
            P("tok"),
            P("tok", None),
        ),
        out_specs=P("tok", "head"),
        check_vma=False,
    )
```

profile of v0, /device:TPU:0, one launch (start us, length us, event | category | flops | bytes accessed | tf_op | source)
XLA Modules:
  0.0 326.8 jit_solution(5233259194347587076)
XLA Ops:
  6.5 0.0 copy-start
  6.5 0.0 copy-start.8
  6.5 0.0 copy-start.6
  6.5 0.0 copy-start.3
  6.5 0.0 copy-start.5
  6.5 0.0 all-gather.3.cloned.1.call-start
  6.6 0.7 all-gather.3.cloned.1.call-update
  7.3 0.0 all-gather.5.cloned.1.call-start
  7.3 0.7 all-gather.5.cloned.1.call-update
  8.0 0.0 reduce-scatter.2.cloned.1.call-start
  8.1 0.0 copy-done.8
  8.1 0.7 dynamic_slice.16
  10.1 0.0 copy-done.6
  10.1 0.1 copy.82
  10.2 0.0 copy-done.3
  10.2 0.2 fusion.34
  10.4 0.0 copy-done.5
  10.4 8.2 %fusion.38 = f32[128,8,512]{2,0,1:T(8,128)S(1)} fusion(bf16[8,2048,512]{2,1,0:T(8,128)(2,1)} %param.18, bf16[128,2048]{1,0:T(8,128)(2,1)S(1)} %copy-done.3, f32[2048]{0:T(1024)S(1)} %copy-done.5, f32[128]{0:T(128)S(1)} %add_rsqrt_fusion), kind=kOutput, calls=%fused_computation.39 | convolution fusion | flops 2148532224 | bytes 19407360 | tf_op jit(solution)/shard_map/td,edc->tec/dot_general | solution.py:77
  18.6 3.1 fusion.11
  21.7 1.7 reshape.339
  23.4 0.0 copy-done
  23.4 0.5 fusion.59
  23.9 0.0 copy-start.7
  23.9 0.1 reshape.340
  24.6 2.1 convolution_convert_fusion
  26.7 0.8 copy.108
  27.5 0.1 copy.83
  27.6 0.1 reshape.360
  27.7 0.0 copy-done.7
  27.8 0.3 fusion.62
  28.1 1.6 gather_fusion
  29.6 0.1 reshape.363
  29.8 0.1 copy.84
  30.6 0.7 compare_and_fusion
  31.3 0.1 fusion.47
  31.4 0.3 multiply_cosine_fusion
  31.7 0.2 fusion.68
  31.9 0.1 subtract_convert_fusion.1
  32.0 0.3 fusion.67
  32.4 0.2 subtract_convert_fusion
  32.6 0.4 fusion.69
  32.9 0.1 fusion.40
  33.0 0.2 iota_compare_fusion
  33.3 103.9 %all-gather.3.cloned.1.call-done = bf16[64,128,512]{2,1,0:T(8,128)(2,1)} async-done(((bf16[8,128,512]{2,1,0:T(8,128)(2,1)}), bf16[64,128,512]{2,1,0:T(8,128)(2,1)}) %all-gather.3.cloned.1.call-update) | async-done | bytes 8388624 | tf_op jit(solution)/shard_map/all_gather | solution.py:109
  137.2 4.1 %gather_fusion.1 = bf16[16,128,512]{2,1,0:T(8,128)(2,1)S(1)} fusion(bf16[64,128,512]{2,1,0:T(8,128)(2,1)} %all-gather.3.cloned.1.call-done, s32[1024]{0:T(1024)S(1)} %pad_clamp_fusion), kind=kCustom, calls=%fused_computation.clone | custom fusion | bytes 4194368 | tf_op jit(solution)/shard_map/while/body/eval_jaxpr/jit(_take)/gather | solution.py:119
  141.2 121.2 %all-gather.5.cloned.1.call-done = bf16[64,128,512]{2,1,0:T(8,128)(2,1)} async-done(((bf16[8,128,512]{2,1,0:T(8,128)(2,1)}), bf16[64,128,512]{2,1,0:T(8,128)(2,1)}) %all-gather.5.cloned.1.call-update) | async-done | bytes 8388624 | tf_op jit(solution)/shard_map/all_gather | solution.py:108
  262.4 5.4 %gather_fusion.2 = bf16[16,128,512]{2,1,0:T(8,128)(2,1)} fusion(bf16[64,128,512]{2,1,0:T(8,128)(2,1)} %all-gather.5.cloned.1.call-done, s32[1024]{0:T(1024)S(1)} %pad_clamp_fusion), kind=kCustom, calls=%fused_computation.1.clone | custom fusion | bytes 4194368 | tf_op jit(solution)/shard_map/while/body/eval_jaxpr/jit(_take)/gather | solution.py:118
  267.8 4.0 %broadcast_select_fusion.1 = (bf16[16,128,512]{2,1,0:T(8,128)(2,1)}, bf16[16,128,512]{2,1,0:T(8,128)(2,1)}) fusion(bf16[16,128,512]{2,1,0:T(8,128)(2,1)S(1)} %gather_fusion.1, pred[16]{0:T(512)(128)(4,1)S(1)} %get-tuple-element.64, bf16[16,128,512]{2,1,0:T(8,128)(2,1)} %gather_fusion.2), kind=kLoop, calls=%fused_computation.20 | loop fusion | flops 2097152 | bytes 8388624 | tf_op jit(solution)/shard_map/while/body/eval_jaxpr/jit(_take)/select_n | solution.py:119
  271.8 2.5 reshape.338
  274.3 4.6 %bitcast_reduce_fusion = (f32[128,2,4]{0,1,2:T(2,128)S(1)}, f32[4,2048,128,2]{2,1,3,0:T(8,128)}) fusion(bf16[128,2,4,64]{3,0,1,2:T(8,128)(2,1)S(1)} %get-tuple-element.69, bf16[128,2,4,64]{3,0,1,2:T(8,128)(2,1)S(1)} %get-tuple-element.68, bf16[2048,4,128,1]{2,1,0,3:T(4,128)(2,1)S(1)} %bitcast.90), kind=kOutput, calls=%fused_computation.4 | convolution fusion | flops 541588480 | bytes 10752000 | tf_op jit(solution)/shard_map/while/body/eval_jaxpr/while/body/eval_jaxpr/rshd,khd->rshk/dot_general | solution.py:25
  278.9 2.5 reshape.337
  281.4 0.0 copy-start.2
  281.5 4.9 %fusion.1 = f32[128,2,4]{0,1,2:T(2,128)S(1)} fusion(f32[4,2048,128,2]{2,1,3,0:T(8,128)} %get-tuple-element.81, f32[128,2,4]{0,1,2:T(2,128)S(1)} %get-tuple-element.80), kind=kLoop, calls=%fused_computation.6 | loop fusion | flops 6290432 | bytes 8396800 | tf_op jit(solution)/shard_map/while/body/eval_jaxpr/while/body/eval_jaxpr/reduce_sum | solution.py:30
  286.4 0.8 copy-done.2
  287.2 2.1 fusion.24
  289.3 0.0 copy-done.4
  289.3 0.3 fusion.32
  289.7 0.2 copy.96
  289.9 0.9 select_reduce_fusion
  290.8 0.0 copy-start.1
  290.8 9.5 %fusion.7 = bf16[128,2048]{1,0:T(8,128)(2,1)} fusion(bf16[8,512,2048]{2,1,0:T(8,128)(2,1)} %param.21, bf16[128,8,512]{2,1,0:T(8,128)(2,1)S(1)} %select_reduce_fusion), kind=kOutput, calls=%fused_computation.12 | convolution fusion | flops 2147745792 | bytes 18350080 | tf_op jit(solution)/shard_map/tec,ecd->td/dot_general | solution.py:144
  300.2 0.0 reduce-scatter.2.cloned.1.call-update
  300.3 20.0 %reduce-scatter.2.cloned.1.call-done = bf16[128,512]{1,0:T(8,128)(2,1)} async-done(((bf16[128,2048]{1,0:T(8,128)(2,1)}), bf16[128,512]{1,0:T(8,128)(2,1)}) %reduce-scatter.2.cloned.1.call-update) | async-done | bytes 131088 | tf_op jit(solution)/shard_map/reduce_scatter | solution.py:145
  320.2 0.0 copy-done.1
  (13 shorter events, 0.2 us)
Async XLA Ops:
  6.5 16.8 %copy-start = (bf16[2048,512]{1,0:T(8,128)(2,1)S(1)}, bf16[2048,512]{1,0:T(8,128)(2,1)}, u32[]{:S(2)}) copy-start(bf16[2048,512]{1,0:T(8,128)(2,1)} %param.19) | copy-start | bytes 6291460
  6.5 1.5 copy-start.8
  6.5 3.6 %copy-start.6 = (s32[128,2]{0,1:T(2,128)S(1)}, s32[128,2]{0,1:T(2,128)}, u32[]{:S(2)}) copy-start(s32[128,2]{0,1:T(2,128)} %param.27) | copy-start | bytes 3076
  6.5 3.7 %copy-start.3 = (bf16[128,2048]{1,0:T(8,128)(2,1)S(1)}, bf16[128,2048]{1,0:T(8,128)(2,1)}, u32[]{:S(2)}) copy-start(bf16[128,2048]{1,0:T(8,128)(2,1)} %param.15) | copy-start | bytes 1572868
  6.5 3.9 %copy-start.5 = (f32[2048]{0:T(1024)S(1)}, f32[2048]{0:T(1024)}, u32[]{:S(2)}) copy-start(f32[2048]{0:T(1024)} %param.16) | copy-start | bytes 24580
  6.5 130.6 %all-gather.3.cloned.1.call-start = ((), (), s32[]{:S(2)}) async-start(), calls=%async_computation.1 | async-start | bytes 9437184 | tf_op jit(solution)/shard_map/all_gather | solution.py:109
  7.3 255.2 %all-gather.5.cloned.1.call-start = ((), (), s32[]{:S(2)}) async-start(), calls=%async_computation.2 | async-start | bytes 9437184 | tf_op jit(solution)/shard_map/all_gather | solution.py:108
  8.0 312.2 %reduce-scatter.2.cloned.1.call-start = ((), (), s32[]{:S(2)}) async-start(), calls=%async_computation.3 | async-start | bytes 655360 | tf_op jit(solution)/shard_map/reduce_scatter | solution.py:145
  23.9 3.9 %copy-start.7 = (bf16[2048,8]{0,1:T(8,128)(2,1)S(1)}, bf16[2048,8]{0,1:T(8,128)(2,1)}, u32[]{:S(2)}) copy-start(bf16[2048,8]{0,1:T(8,128)(2,1)} %param.17) | copy-start | bytes 98308
  281.4 5.8 %copy-start.2 = (f32[4,2048,128,2]{2,1,3,0:T(8,128)S(1)}, f32[4,2048,128,2]{2,1,3,0:T(8,128)}, u32[]{:S(2)}) copy-start(f32[4,2048,128,2]{2,1,3,0:T(8,128)} %get-tuple-element.81) | copy-start | bytes 25165828
  287.2 2.1 copy-start.4
  290.8 29.5 %copy-start.1 = (bf16[2048,512]{1,0:T(8,128)(2,1)S(1)}, bf16[2048,512]{1,0:T(8,128)(2,1)}, u32[]{:S(2)}) copy-start(bf16[2048,512]{1,0:T(8,128)(2,1)} %param.19) | copy-start | bytes 6291460
Sparse Core Ops, SparseCore 0:
  9.5 127.6 all-gather.2
  139.3 123.1 all-gather.4
  300.4 19.8 reduce-scatter.1
where the time goes:
time: 327 us
  waiting for transfers between devices  246 us (75%)
  matrix products  30.9 us (9%)
  local copies, waits for them, and re-layouts  21.4 us (7%)
  between operations  16.1 us (5%)
  other arithmetic  11.8 us (4%)
    all_gather x1, waiting for transfers between devices, per_device(): lax.all_gather(key_pool, 'tok', axis=0, tiled=True)  121 us
    all_gather x1, waiting for transfers between devices, per_device(): lax.all_gather(value_pool, 'tok', axis=0, tiled=True)  104 us
    reduce_scatter x1, waiting for transfers between devices, per_device(): lax.psum_scatter(partial_out.astype(jnp.bfloat16), 'head', scatter_dimens...  20 us
    dot_general x1, matrix products, per_device(): jnp.einsum('tec,ecd->td', picked, w_out, preferred_element_type=jnp.float32)  9.46 us
    dot_general x1, matrix products, per_device(): jnp.einsum('td,edc->tec', normed, w_query, preferred_element_type=jnp.flo...  8.21 us
  transfers between devices with their start and end apart: 3, of which 3 were waited for; matrix products, arithmetic and copies ran while one was open for 8% of the time, Pallas kernels for 0%

commit v1 on v0

v1 whole, which is shorter than its diff:
```python
import functools

import jax
import jax.numpy as jnp
import numpy as np
from jax import lax
from jax.experimental import pallas as pl
from jax.experimental.pallas import tpu as pltpu
from jax.sharding import PartitionSpec as P

HD = 128
F32 = jnp.float32
BF16 = jnp.bfloat16
NEG = -1e30
NBUF = 4
MESH = pl.DeviceIdType.MESH


def rope_tables(rows, first):
    half = HD // 2
    freq = (10000.0 ** (-np.arange(half, dtype=np.float64) * 2.0 / HD)).astype(np.float32)
    angle = (np.arange(rows, dtype=np.float32)[:, None] + np.float32(first)) * freq[None, :]
    cosine, sine = np.cos(angle), np.sin(angle)
    return (
        np.concatenate([cosine, cosine], axis=1).astype(np.float32),
        np.concatenate([-sine, sine], axis=1).astype(np.float32),
    )


def project_kernel(
    hidden, gain, router, att, cos, sin, wq, wk, wv,
    q_out, k_out, vt_out, gate_out,
    wbuf, kvbuf, normed, qacc, sems, kvsems,
):
    experts, _, cols = wq.shape
    heads = cols // HD
    rows = hidden.shape[0]
    topk = att.shape[1]

    def fetch(e, slot):
        return pltpu.make_async_copy(wq.at[e], wbuf.at[slot], sems.at[slot])

    for e in range(NBUF):
        fetch(e, e).start()
    fetch_k = pltpu.make_async_copy(wk, kvbuf.at[0], kvsems.at[0])
    fetch_v = pltpu.make_async_copy(wv, kvbuf.at[1], kvsems.at[1])
    fetch_k.start()
    fetch_v.start()

    state = hidden[...].astype(F32)
    inv = lax.rsqrt(jnp.mean(state * state, axis=-1, keepdims=True) + 1e-06)
    normed[...] = (state * inv * gain[...]).astype(BF16)
    logits = jnp.dot(normed[...], router[...], preferred_element_type=F32)
    lane = lax.broadcasted_iota(jnp.int32, logits.shape, 1)
    picks = [
        jnp.sum(jnp.where(lane == att[:, s : s + 1], logits, 0.0), axis=1, keepdims=True)
        for s in range(topk)
    ]
    top = functools.reduce(jnp.maximum, picks)
    raised = [jnp.exp(x - top) for x in picks]
    total = functools.reduce(jnp.add, raised)
    for s in range(topk):
        gate_out[s * rows : (s + 1) * rows, :] = raised[s] / total
    qacc[...] = jnp.zeros_like(qacc)

    def step(e, carry):
        slot = lax.rem(e, NBUF)
        fetch(e, slot).wait()
        prod = jnp.dot(normed[...], wbuf[slot], preferred_element_type=F32)
        for s in range(topk):
            qacc[s] = jnp.where(att[:, s : s + 1] == e, prod, qacc[s])

        @pl.when(e + NBUF < experts)
        def _():
            fetch(e + NBUF, slot).start()

        return carry

    lax.fori_loop(0, experts, step, 0)

    def rope(u):
        return u * cos[...] + pltpu.roll(u, HD // 2, 1) * sin[...]

    for h in range(heads):
        for s in range(topk):
            q_out[h, s * rows : (s + 1) * rows, :] = rope(
                qacc[s, :, h * HD : (h + 1) * HD]
            ).astype(BF16)
    fetch_k.wait()
    keys = jnp.dot(normed[...], kvbuf[0], preferred_element_type=F32)
    for h in range(heads):
        k_out[h] = rope(keys[:, h * HD : (h + 1) * HD]).astype(BF16)
    fetch_v.wait()
    vals = jnp.dot(normed[...], kvbuf[1], preferred_element_type=F32)
    for h in range(heads):
        vt_out[h] = vals[:, h * HD : (h + 1) * HD].T.astype(BF16)


def attend_kernel(
    tok_bits, head_bits, units,
    meta, length, q_in, k_in, vt_in, gates, att, kpool, vpool, wout,
    out,
    *scratch,
):
    heads, qrows, _ = q_in.shape
    suffix = k_in.shape[1]
    topk = qrows // suffix
    pages = kpool.shape[0]
    rounds = len(tok_bits)
    half = 2 ** (rounds - 1)
    experts = wout.shape[0] // (heads * HD)
    scale = 1.0 / HD**0.5
    blocks = 2 ** len(head_bits)
    width = wout.shape[1] // blocks

    it = iter(scratch)
    qall = [next(it) for _ in range(heads)]
    sbuf = [[next(it) for _ in range(rounds)] for _ in range(heads)]
    sstat = [[next(it) for _ in range(rounds)] for _ in range(heads)]
    rbuf = [[next(it) for _ in range(rounds)] for _ in range(heads)]
    rstat = [[next(it) for _ in range(rounds)] for _ in range(heads)]
    vt = next(it)
    ust = next(it)
    ustat = next(it)
    cur = next(it)
    cstat = next(it)
    wbuf = next(it)
    picked = next(it)
    osend = [next(it) for _ in head_bits]
    orecv = [next(it) for _ in head_bits]
    oacc = next(it)
    ag_s, ag_r = next(it), next(it)
    rs_s, rs_r = next(it), next(it)
    rt_s, rt_r = next(it), next(it)
    o_s, o_r = next(it), next(it)
    w_sem = next(it)
    q_sem = next(it)

    tok = lax.axis_index("tok")
    head = lax.axis_index("head")

    def flip(index, bit):
        return index + bit * (1 - 2 * ((index // bit) % 2))

    partners = [{"tok": flip(tok, b)} for b in tok_bits]
    mates = [{"head": flip(head, b)} for b in head_bits]

    barrier = pltpu.get_barrier_semaphore()
    for other in partners + mates:
        pl.semaphore_signal(barrier, inc=1, device_id=other, device_id_type=MESH)

    def block_of(j):
        col = head
        for n, b in enumerate(head_bits):
            if (j >> n) & 1:
                col = flip(col, b)
        return col

    local_q = []
    for h in range(heads):
        c = pltpu.make_async_copy(q_in.at[h], qall[h].at[0], q_sem.at[h])
        c.start()
        local_q.append(c)
    loads = []
    for j in range(blocks):
        c = pltpu.make_async_copy(
            wout.at[:, pl.ds(pl.multiple_of(block_of(j) * width, 128), width)],
            wbuf.at[j],
            w_sem.at[j],
        )
        c.start()
        loads.append(c)
    pl.semaphore_wait(barrier, len(partners) + len(mates))

    def gather_copy(h, k):
        n = 2**k
        return pltpu.make_async_remote_copy(
            src_ref=qall[h].at[pl.ds(0, n)],
            dst_ref=qall[h].at[pl.ds(n, n)],
            send_sem=ag_s.at[h, k],
            recv_sem=ag_r.at[h, k],
            device_id=partners[k],
            device_id_type=MESH,
        )

    for h in range(heads):
        local_q[h].wait()
        gather_copy(h, 0).start()
    for p in range(pages):
        for h in range(heads):
            vt[h, p] = vpool[p, :, h * HD : (h + 1) * HD].T
    ust[0] = jnp.zeros_like(ust[0])
    ustat[0, 0:1] = jnp.full((1, qrows), NEG, F32)
    ustat[0, 1:2] = jnp.zeros((1, qrows), F32)
    for k in range(1, rounds):
        for h in range(heads):
            gather_copy(h, k - 1).wait_recv()
            gather_copy(h, k).start()

    def scores_t(keys, queries):
        return (
            lax.dot_general(
                keys, queries, (((1,), (1,)), ((), ())), preferred_element_type=F32
            )
            * scale
        )

    def attend(h):
        def unit(u, carry):
            req, page, same = meta[0, u], meta[1, u], meta[2, u]
            s = scores_t(kpool[page, :, h * HD : (h + 1) * HD], qall[h][req])
            m_old = jnp.where(same == 1, ustat[u, 0:1], NEG)
            m_new = jnp.maximum(m_old, jnp.max(s, axis=0, keepdims=True))
            alpha = jnp.exp(m_old - m_new)
            w = jnp.exp(s - m_new)
            ustat[u + 1, 0:1] = m_new
            ustat[u + 1, 1:2] = ustat[u, 1:2] * alpha + jnp.sum(w, axis=0, keepdims=True)
            ust[u + 1] = ust[u] * alpha + jnp.dot(
                vt[h, page], w.astype(BF16), preferred_element_type=F32
            )
            return carry

        lax.fori_loop(0, units, unit, 0)

        def keep(i, carry):
            cur[h, i] = ust[meta[3, i]]
            cstat[h, i] = ustat[meta[3, i]]
            return carry

        lax.fori_loop(0, half, keep, 0)

        def give(i, carry):
            sbuf[h][0][i] = ust[meta[3, half + i]].astype(BF16)
            sstat[h][0][i] = ustat[meta[3, half + i]]
            return carry

        lax.fori_loop(0, half, give, 0)

    def reduce_copies(h, k):
        bit = rounds - 1 - k
        return (
            pltpu.make_async_remote_copy(
                src_ref=sbuf[h][k], dst_ref=rbuf[h][k],
                send_sem=rs_s.at[h, k], recv_sem=rs_r.at[h, k],
                device_id=partners[bit], device_id_type=MESH,
            ),
            pltpu.make_async_remote_copy(
                src_ref=sstat[h][k], dst_ref=rstat[h][k],
                send_sem=rt_s.at[h, k], recv_sem=rt_r.at[h, k],
                device_id=partners[bit], device_id_type=MESH,
            ),
        )

    def merged(m_a, l_a, o_a, m_b, l_b, o_b):
        m = jnp.maximum(m_a, m_b)
        a, b = jnp.exp(m_a - m), jnp.exp(m_b - m)
        return m, l_a * a + l_b * b, o_a * a + o_b * b

    def merge_at(h, k, i):
        return merged(
            cstat[h, i, 0:1], cstat[h, i, 1:2], cur[h, i],
            rstat[h][k][i, 0:1], rstat[h][k][i, 1:2], rbuf[h][k][i].astype(F32),
        )

    for h in range(heads):
        gather_copy(h, rounds - 1).wait_recv()
        attend(h)
        for c in reduce_copies(h, 0):
            c.start()

    slot = lax.broadcasted_iota(jnp.int32, (suffix, qrows), 1) % suffix
    key_at = lax.broadcasted_iota(jnp.int32, (suffix, qrows), 0)
    mask = (key_at <= slot) & (key_at < length[0])

    for k in range(rounds - 1):
        n = 2 ** (rounds - 2 - k)
        for h in range(heads):
            for c in reduce_copies(h, k):
                c.wait_recv()

            def give(i, carry, h=h, k=k, n=n):
                m, l, o = merge_at(h, k, n + i)
                sstat[h][k + 1][i, 0:1] = m
                sstat[h][k + 1][i, 1:2] = l
                sbuf[h][k + 1][i] = o.astype(BF16)
                return carry

            lax.fori_loop(0, n, give, 0)
            for c in reduce_copies(h, k + 1):
                c.start()

            def keep(i, carry, h=h, k=k):
                m, l, o = merge_at(h, k, i)
                cstat[h, i, 0:1] = m
                cstat[h, i, 1:2] = l
                cur[h, i] = o
                return carry

            lax.fori_loop(0, n, keep, 0)
            if k == 0:
                s = jnp.where(mask, scores_t(k_in[h], q_in[h]), NEG)
                m_s = jnp.max(s, axis=0, keepdims=True)
                w = jnp.exp(s - m_s)
                l_s = jnp.sum(w, axis=0, keepdims=True)
                o_s_ = jnp.dot(vt_in[h], w.astype(BF16), preferred_element_type=F32)
                m, l, o = merged(
                    cstat[h, 0, 0:1], cstat[h, 0, 1:2], cur[h, 0], m_s, l_s, o_s_
                )
                cstat[h, 0, 0:1] = m
                cstat[h, 0, 1:2] = l
                cur[h, 0] = o

    row = lax.broadcasted_iota(jnp.int32, (qrows, 1), 0) % suffix
    factor = gates[...] * (row < length[0]).astype(F32)
    for h in range(heads):
        for c in reduce_copies(h, rounds - 1):
            c.wait_recv()
        m, l, o = merge_at(h, rounds - 1, 0)
        weighted = ((o / l).T * factor).astype(F32)
        for e in range(experts):
            value = jnp.zeros((suffix, HD), F32)
            for s in range(topk):
                value = jnp.where(
                    att[:, s : s + 1] == e, weighted[s * suffix : (s + 1) * suffix], value
                )
            picked[:, (e * heads + h) * HD : (e * heads + h + 1) * HD] = value.astype(BF16)

    depth = heads * HD

    def multiply(j):
        loads[j].wait()
        oacc[...] = jnp.zeros_like(oacc)

        def part(e, carry):
            at = pl.ds(pl.multiple_of(e * depth, depth), depth)
            oacc[...] += jnp.dot(picked[:, at], wbuf[j, at, :], preferred_element_type=F32)
            return carry

        lax.fori_loop(0, experts, part, 0)
        return oacc[...]

    def out_copy(k):
        return pltpu.make_async_remote_copy(
            src_ref=osend[k], dst_ref=orecv[k],
            send_sem=o_s.at[k], recv_sem=o_r.at[k],
            device_id=mates[len(head_bits) - 1 - k], device_id_type=MESH,
        )

    levels = len(head_bits)
    for j in range(blocks // 2, blocks):
        osend[0][j - blocks // 2] = multiply(j).astype(BF16)
    out_copy(0).start()
    for k in range(1, levels):
        n = 2 ** (levels - 1 - k)
        own = [multiply(j) for j in range(n, 2 * n)]
        out_copy(k - 1).wait_recv()
        for j in range(n):
            total = own[j]
            for i in range(k):
                total = total + orecv[i][n + j].astype(F32)
            osend[k][j] = total.astype(BF16)
        out_copy(k).start()
    total = multiply(0)
    out_copy(levels - 1).wait_recv()
    for i in range(levels):
        total = total + orecv[i][0].astype(F32)
    out[...] = total.astype(BF16)

    for k in range(levels):
        out_copy(k).wait_send()
    for h in range(heads):
        for k in range(rounds):
            gather_copy(h, k).wait_send()
            for c in reduce_copies(h, k):
                c.wait_send()


def unit_table(page_table, request_group, deltas, local_pages):
    groups, per_group = page_table.shape
    requests = request_group.shape[0]
    units = local_pages * (requests // groups)
    tok = lax.axis_index("tok")
    order = jnp.bitwise_xor(tok, jnp.asarray(deltas, jnp.int32))
    number = jnp.arange(requests, dtype=jnp.int32)
    group_of = jnp.sum(
        jnp.where(order[:, None] == number[None, :], request_group[None, :], 0), axis=1
    )
    mine = tok * local_pages + jnp.arange(local_pages, dtype=jnp.int32)
    flat = page_table.reshape(-1)
    owner = jnp.arange(flat.shape[0], dtype=jnp.int32) // per_group
    page_group = jnp.sum(jnp.where(flat[None, :] == mine[:, None], owner[None, :], 0), axis=1)
    uses = (group_of[:, None] == page_group[None, :]).astype(jnp.int32).reshape(-1)
    count = uses.shape[0]
    place = jnp.arange(count, dtype=jnp.int32)
    running = jnp.sum(jnp.where(place[None, :] <= place[:, None], uses[None, :], 0), axis=1)
    at = jnp.sum(
        (running[None, :] <= jnp.arange(units, dtype=jnp.int32)[:, None]).astype(jnp.int32), axis=1
    )
    req, page = at // local_pages, at % local_pages
    before = jnp.concatenate([jnp.full((1,), -1, jnp.int32), req[:-1]])
    per = uses.reshape(requests, local_pages)
    ends = running.reshape(requests, local_pages)[:, -1]
    last = jnp.where(jnp.sum(per, axis=1) > 0, ends, 0)
    size = max(units, requests)
    pad = lambda x: jnp.pad(x, (0, size - x.shape[0]))
    return jnp.stack([pad(req), pad(page), pad((req == before).astype(jnp.int32)), pad(last)])


def per_device(
    toks, heads_dev,
    hidden, norm_gain, w_router, w_query, w_key, w_value, w_out,
    key_pool, value_pool, page_table, request_group, suffix_len, att_experts,
):
    rows, model = hidden.shape
    cols = w_key.shape[1]
    heads = cols // HD
    topk = att_experts.shape[1]
    experts = w_query.shape[0]
    prefix = page_table.shape[1] * key_pool.shape[1]
    pages = key_pool.shape[0]
    requests = request_group.shape[0]
    page_rows = key_pool.shape[1]
    qrows = topk * rows
    x = max(toks // 4, 1)
    bits = [1 << n for n in range(toks.bit_length() - 1)]
    tok_bits = [b for b in bits if b >= x] + [b for b in bits if b < x]
    rounds = len(tok_bits)
    deltas = [
        sum(b for n, b in enumerate(tok_bits) if (i >> n) & 1) for i in range(toks)
    ]
    head_bits = [1 << n for n in range(1, heads_dev.bit_length() - 1)] + [1]
    levels = len(head_bits)
    units = pages * (requests // page_table.shape[0])
    meta = unit_table(page_table, request_group, deltas, pages)
    cos, sin = rope_tables(rows, prefix)
    vm = pl.BlockSpec(memory_space=pltpu.VMEM)
    sm = pl.BlockSpec(memory_space=pltpu.SMEM)
    hbm = pl.BlockSpec(memory_space=pl.ANY)
    q, k, vt, gates = pl.pallas_call(
        project_kernel,
        out_shape=(
            jax.ShapeDtypeStruct((heads, qrows, HD), BF16),
            jax.ShapeDtypeStruct((heads, rows, HD), BF16),
            jax.ShapeDtypeStruct((heads, HD, rows), BF16),
            jax.ShapeDtypeStruct((qrows, 1), F32),
        ),
        in_specs=[vm] * 6 + [hbm] * 3,
        out_specs=(vm,) * 4,
        scratch_shapes=[
            pltpu.VMEM((NBUF, model, cols), BF16),
            pltpu.VMEM((2, model, cols), BF16),
            pltpu.VMEM((rows, model), BF16),
            pltpu.VMEM((topk, rows, cols), F32),
            pltpu.SemaphoreType.DMA((NBUF,)),
            pltpu.SemaphoreType.DMA((2,)),
        ],
        compiler_params=pltpu.CompilerParams(vmem_limit_bytes=40 * 2**20),
        name="project",
    )(
        hidden, norm_gain.reshape(1, -1), w_router, att_experts,
        jnp.asarray(cos), jnp.asarray(sin), w_query, w_key, w_value,
    )
    sizes = [2 ** (rounds - 1 - k_) for k_ in range(rounds)]
    width = model // heads_dev
    dma = pltpu.SemaphoreType.DMA
    scratch = (
        [pltpu.VMEM((toks, qrows, HD), BF16) for _ in range(heads)]
        + [pltpu.VMEM((n, HD, qrows), BF16) for _ in range(heads) for n in sizes]
        + [pltpu.VMEM((n, 2, qrows), F32) for _ in range(heads) for n in sizes]
        + [pltpu.VMEM((n, HD, qrows), BF16) for _ in range(heads) for n in sizes]
        + [pltpu.VMEM((n, 2, qrows), F32) for _ in range(heads) for n in sizes]
        + [
            pltpu.VMEM((heads, pages, HD, page_rows), BF16),
            pltpu.VMEM((units + 1, HD, qrows), F32),
            pltpu.VMEM((units + 1, 2, qrows), F32),
            pltpu.VMEM((heads, sizes[0], HD, qrows), F32),
            pltpu.VMEM((heads, sizes[0], 2, qrows), F32),
            pltpu.VMEM((heads_dev, experts * cols, width), BF16),
            pltpu.VMEM((rows, experts * cols), BF16),
        ]
        + [pltpu.VMEM((2 ** (levels - 1 - k_), rows, width), BF16) for k_ in range(levels)] * 2
        + [
            pltpu.VMEM((rows, width), F32),
            dma((heads, rounds)), dma((heads, rounds)),
            dma((heads, rounds)), dma((heads, rounds)),
            dma((heads, rounds)), dma((heads, rounds)),
            dma((levels,)), dma((levels,)),
            dma((heads_dev,)), dma((heads,)),
        ]
    )
    return pl.pallas_call(
        functools.partial(attend_kernel, tok_bits, head_bits, units),
        out_shape=jax.ShapeDtypeStruct((rows, width), BF16),
        in_specs=[sm, sm] + [vm] * 7 + [hbm],
        out_specs=vm,
        scratch_shapes=scratch,
        compiler_params=pltpu.CompilerParams(
            collective_id=0, has_side_effects=True, vmem_limit_bytes=56 * 2**20
        ),
        name="attend",
    )(
        meta, suffix_len, q, k, vt, gates, att_experts, key_pool, value_pool,
        w_out.reshape(experts * cols, model),
    )


def solution(mesh):
    return jax.shard_map(
        functools.partial(per_device, mesh.shape["tok"], mesh.shape["head"]),
        mesh=mesh,
        in_specs=(
            P("tok", None), P(), P(), P(None, None, "head"), P(None, "head"), P(None, "head"),
            P(None, "head", None), P("tok", None, "head"), P("tok", None, "head"),
            P(), P(), P("tok"), P("tok", None),
        ),
        out_specs=P("tok", "head"),
        check_vma=False,
    )
```

time: 327 us -> 116 us (0.35)
  waiting for transfers between devices: 246 us -> 0 us
  Pallas kernels: 0 us -> 98 us
  matrix products: 30.9 us -> 0 us
  between operations: 16.1 us -> 0.76 us
  other arithmetic: 11.8 us -> 2.86 us
  local copies, waits for them, and re-layouts: 21.4 us -> 13.8 us
    all_gather x2 -> x0, waiting for transfers between devices: 225 us -> none  [the longest x1 121 us: per_device(): lax.all_gather(key_pool, 'tok', axis=0, tiled=True)]
    pallas_call x0 -> x2, Pallas kernels: none -> 98 us  [the longest x1 90.1 us: per_device(): pl.pallas_call(functools.partial(attend_kernel, tok_bits, head_bits, unit...]
    dot_general x10 -> x0, matrix products: 30.9 us -> none  [the longest x1 9.46 us: per_device(): jnp.einsum('tec,ecd->td', picked, w_out, preferred_element_type=jnp.float32)]
    reduce_scatter x1 -> x0, waiting for transfers between devices: 20 us -> none  [per_device(): lax.psum_scatter(partial_out.astype(jnp.bfloat16), 'head', scatter_dimens...]
    unnamed x19 -> x25, local copies, waits for them, and re-layouts: 0.99 us -> 12.6 us
    gather x7 -> x0, local copies, waits for them, and re-layouts: 11.4 us -> none  [the longest x1 5.37 us: one_request(): jnp.take(all_keys, pages, axis=0).reshape(prefix_len, local_heads, HD)]
    reshape x4 -> x1, local copies, waits for them, and re-layouts: 6.83 us -> 0.08 us  [unit_table(): ends = running.reshape(requests, local_pages)[:, -1]]
    reduce_sum x5, other arithmetic: 6.09 us -> 1.43 us  [the longest x1 0.84 us: unit_table(): jnp.sum(jnp.where(order[:, None] == number[None, :], request_group[None,...]
  transfers between devices with their start and end apart: 3 -> 0, of which waited for: 3 -> 0; matrix products, arithmetic and copies ran while one was open for 8% -> 0% of each run, Pallas kernels for 0% -> 0%
where the time goes in v1:
time: 116 us; the launch traced here: 115 us
  Pallas kernels  98 us (84%)
  local copies, waits for them, and re-layouts  13.8 us (12%)
  other arithmetic  2.86 us (2%)
    pallas_call x1, Pallas kernels, per_device(): pl.pallas_call(functools.partial(attend_kernel, tok_bits, head_bits, unit...  90.1 us
    unnamed x25, local copies, waits for them, and re-layouts  12.6 us
    pallas_call x1, Pallas kernels, per_device(): pl.pallas_call(project_kernel, out_shape=(jax.ShapeDtypeStruct((heads, qr...  7.87 us

profile of v1, /device:TPU:0, one launch (start us, length us, event | category | flops | bytes accessed | tf_op | source)
XLA Modules:
  0.0 115.4 jit_solution(11938953060031469197)
XLA Ops:
  0.0 0.8 eq.62
  0.8 0.2 select_reduce_fusion.1
  1.0 0.7 broadcast_xor_fusion
  1.6 0.8 select_reduce_fusion.2
  2.5 0.1 compare_convert_fusion
  2.5 0.1 reshape.157
  2.6 0.1 select_reduce_fusion
  2.7 0.1 convert_reduce_fusion
  2.9 0.1 compare_convert_fusion.1
  2.9 0.1 reshape.154
  3.0 0.2 slice_reduce_fusion
  3.2 0.2 fusion
  3.4 0.6 pad_add_fusion.meta
  4.0 0.8 copy.24.att
  4.8 0.0 copy-start.2
  4.8 1.1 copy.23.router
  5.9 0.0 copy-start
  5.9 1.6 %copy-done = bf16[2048,512]{1,0:T(8,128)(2,1)S(1)} copy-done((bf16[2048,512]{1,0:T(8,128)(2,1)S(1)}, bf16[2048,512]{1,0:T(8,128)(2,1)}, u32[]{:S(2)}) %copy-start) | copy-done | bytes 2097176
  7.5 0.0 copy-start.1
  7.5 1.6 %copy-done.1 = bf16[2048,512]{1,0:T(8,128)(2,1)S(1)} copy-done((bf16[2048,512]{1,0:T(8,128)(2,1)S(1)}, bf16[2048,512]{1,0:T(8,128)(2,1)}, u32[]{:S(2)}) %copy-start.1) | copy-done | bytes 2097176
  9.1 0.0 copy-start.3
  9.1 1.0 copy-done.3
  10.1 0.0 copy-start.8
  10.1 0.8 copy-done.8
  10.9 0.0 copy-start.9
  10.9 0.8 copy-done.9
  11.8 0.0 copy-start.10
  11.8 0.7 copy-done.10
  12.5 7.9 %project.1 = (bf16[4,256,128]{2,1,0:T(8,128)(2,1)S(1)}, bf16[4,128,128]{2,1,0:T(8,128)(2,1)S(1)}, bf16[4,128,128]{2,1,0:T(8,128)(2,1)S(1)}, f32[256,1]{1,0:T(8,128)S(1)}) custom-call(bf16[128,2048]{1,0:T(8,128)(2,1)S(1)} %copy-done.3, f32[1,2048]{1,0:T(1,128)S(1)} %bitcast.23, bf16[2048,8]{1,0:T(8,128)(2,1)S(1)} %copy.23.router, s32[128,2]{1,0:T(8,128)S(1)} %copy.24.att, ...), custom_call_target="tpu_custom_call" | custom-call | tf_op jit(solution)/shard_map/project/pallas_call | solution.py:439
  20.4 0.0 copy-start.4
  20.4 0.7 copy-done.4
  21.0 0.0 copy-start.5
  21.1 0.7 copy-done.5
  21.7 0.0 copy-start.6
  21.7 0.7 copy-done.6
  22.4 0.0 copy-start.7
  22.4 0.6 copy-done.7
  23.7 0.0 copy-done.2
  23.7 90.1 %attend.1 = bf16[128,512]{1,0:T(8,128)(2,1)} custom-call(s32[4,16]{1,0:T(4,128)} %pad_add_fusion.meta, s32[1]{0:T(128)S(6)} %copy.27.length, bf16[4,256,128]{2,1,0:T(8,128)(2,1)} %copy-done.4, bf16[4,128,128]{2,1,0:T(8,128)(2,1)} %copy-done.5, bf16[4,128,128]{2,1,0:T(8,128)(2,1)} %copy-done.6, f32[256,1]{1,0:T(8,128)} %copy-done.7, s32[128,2]{1,0:T(8,128)} %copy-done.2, ...), custom_call_target="tpu_custom_call" | custom-call | tf_op jit(solution)/shard_map/attend/pallas_call | solution.py:491
  113.8 1.6 %copy.28 = bf16[128,512]{1,0:T(8,128)(2,1)} copy(bf16[128,512]{1,0:T(8,128)(2,1)} %attend.1) | data formatting | bytes 262144
  (7 shorter events, 0.0 us)
Async XLA Ops:
  4.8 18.9 %copy-start.2 = (s32[128,2]{1,0:T(8,128)}, s32[128,2]{1,0:T(8,128)S(1)}, u32[]{:S(2)}) copy-start(s32[128,2]{1,0:T(8,128)S(1)} %copy.24.att) | copy-start | bytes 3076
  5.9 1.6 %copy-start = (bf16[2048,512]{1,0:T(8,128)(2,1)S(1)}, bf16[2048,512]{1,0:T(8,128)(2,1)}, u32[]{:S(2)}) copy-start(bf16[2048,512]{1,0:T(8,128)(2,1)} %wk.1) | copy-start | bytes 6291460
  7.5 1.6 %copy-start.1 = (bf16[2048,512]{1,0:T(8,128)(2,1)S(1)}, bf16[2048,512]{1,0:T(8,128)(2,1)}, u32[]{:S(2)}) copy-start(bf16[2048,512]{1,0:T(8,128)(2,1)} %wv.1) | copy-start | bytes 6291460
  9.1 1.0 copy-start.3
  10.1 0.8 copy-start.8
  10.9 0.8 copy-start.9
  11.8 0.7 copy-start.10
  20.4 0.7 copy-start.4
  21.0 0.7 copy-start.5
  21.7 0.7 copy-start.6
  22.4 0.7 copy-start.7

commit v2 on v1

--- a/solution.py
+++ b/solution.py
@@ -12,7 +12,6 @@
 F32 = jnp.float32
 BF16 = jnp.bfloat16
 NEG = -1e30
-NBUF = 4
 MESH = pl.DeviceIdType.MESH
 
 
@@ -27,84 +26,16 @@
     )
 
 
-def project_kernel(
-    hidden, gain, router, att, cos, sin, wq, wk, wv,
-    q_out, k_out, vt_out, gate_out,
-    wbuf, kvbuf, normed, qacc, sems, kvsems,
-):
-    experts, _, cols = wq.shape
-    heads = cols // HD
-    rows = hidden.shape[0]
-    topk = att.shape[1]
-
-    def fetch(e, slot):
-        return pltpu.make_async_copy(wq.at[e], wbuf.at[slot], sems.at[slot])
-
-    for e in range(NBUF):
-        fetch(e, e).start()
-    fetch_k = pltpu.make_async_copy(wk, kvbuf.at[0], kvsems.at[0])
-    fetch_v = pltpu.make_async_copy(wv, kvbuf.at[1], kvsems.at[1])
-    fetch_k.start()
-    fetch_v.start()
-
-    state = hidden[...].astype(F32)
-    inv = lax.rsqrt(jnp.mean(state * state, axis=-1, keepdims=True) + 1e-06)
-    normed[...] = (state * inv * gain[...]).astype(BF16)
-    logits = jnp.dot(normed[...], router[...], preferred_element_type=F32)
-    lane = lax.broadcasted_iota(jnp.int32, logits.shape, 1)
-    picks = [
-        jnp.sum(jnp.where(lane == att[:, s : s + 1], logits, 0.0), axis=1, keepdims=True)
-        for s in range(topk)
-    ]
-    top = functools.reduce(jnp.maximum, picks)
-    raised = [jnp.exp(x - top) for x in picks]
-    total = functools.reduce(jnp.add, raised)
-    for s in range(topk):
-        gate_out[s * rows : (s + 1) * rows, :] = raised[s] / total
-    qacc[...] = jnp.zeros_like(qacc)
-
-    def step(e, carry):
-        slot = lax.rem(e, NBUF)
-        fetch(e, slot).wait()
-        prod = jnp.dot(normed[...], wbuf[slot], preferred_element_type=F32)
-        for s in range(topk):
-            qacc[s] = jnp.where(att[:, s : s + 1] == e, prod, qacc[s])
-
-        @pl.when(e + NBUF < experts)
-        def _():
-            fetch(e + NBUF, slot).start()
-
-        return carry
-
-    lax.fori_loop(0, experts, step, 0)
-
-    def rope(u):
-        return u * cos[...] + pltpu.roll(u, HD // 2, 1) * sin[...]
-
-    for h in range(heads):
-        for s in range(topk):
-            q_out[h, s * rows : (s + 1) * rows, :] = rope(
-                qacc[s, :, h * HD : (h + 1) * HD]
-            ).astype(BF16)
-    fetch_k.wait()
-    keys = jnp.dot(normed[...], kvbuf[0], preferred_element_type=F32)
-    for h in range(heads):
-        k_out[h] = rope(keys[:, h * HD : (h + 1) * HD]).astype(BF16)
-    fetch_v.wait()
-    vals = jnp.dot(normed[...], kvbuf[1], preferred_element_type=F32)
-    for h in range(heads):
-        vt_out[h] = vals[:, h * HD : (h + 1) * HD].T.astype(BF16)
-
-
 def attend_kernel(
     tok_bits, head_bits, units,
-    meta, length, q_in, k_in, vt_in, gates, att, kpool, vpool, wout,
+    meta, length, hidden, gain, router, att, cos, sin, kpool, vpool, wq, wk, wv, wout,
     out,
     *scratch,
 ):
-    heads, qrows, _ = q_in.shape
-    suffix = k_in.shape[1]
-    topk = qrows // suffix
+    suffix = hidden.shape[0]
+    topk = att.shape[1]
+    qrows = topk * suffix
+    heads = wk.shape[1] // HD
     pages = kpool.shape[0]
     rounds = len(tok_bits)
     half = 2 ** (rounds - 1)
@@ -135,6 +66,8 @@
     o_s, o_r = next(it), next(it)
     w_sem = next(it)
     q_sem = next(it)
+    kv_sem = next(it)
+    wqbuf, kvbuf, normed, qacc, k_in, vt_in, gates = [next(it) for _ in range(7)]
 
     tok = lax.axis_index("tok")
     head = lax.axis_index("head")
@@ -156,20 +89,72 @@
                 col = flip(col, b)
         return col
 
-    local_q = []
-    for h in range(heads):
-        c = pltpu.make_async_copy(q_in.at[h], qall[h].at[0], q_sem.at[h])
-        c.start()
-        local_q.append(c)
-    loads = []
-    for j in range(blocks):
-        c = pltpu.make_async_copy(
+    def fetch_q(h):
+        return pltpu.make_async_copy(
+            wq.at[:, :, pl.ds(h * HD, HD)], wqbuf.at[h % 2], q_sem.at[h % 2]
+        )
+
+    fetch_k = pltpu.make_async_copy(wk, kvbuf.at[0], kv_sem.at[0])
+    fetch_v = pltpu.make_async_copy(wv, kvbuf.at[1], kv_sem.at[1])
+    loads = [
+        pltpu.make_async_copy(
             wout.at[:, pl.ds(pl.multiple_of(block_of(j) * width, 128), width)],
             wbuf.at[j],
             w_sem.at[j],
         )
-        c.start()
-        loads.append(c)
+        for j in range(blocks)
+    ]
+    for h in range(min(2, heads)):
+        fetch_q(h).start()
+
+    state = hidden[...].astype(F32)
+    inv = lax.rsqrt(jnp.mean(state * state, axis=-1, keepdims=True) + 1e-06)
+    normed[...] = (state * inv * gain[...]).astype(BF16)
+
+    def rope(u):
+        return u * cos[...] + pltpu.roll(u, HD // 2, 1) * sin[...]
+
+    def project(h):
+        fetch_q(h).wait()
+        qacc[...] = jnp.zeros_like(qacc)
+
+        def step(e, carry):
+            prod = jnp.dot(normed[...], wqbuf[h % 2, e], preferred_element_type=F32)
+            for s in range(topk):
+                qacc[s] = jnp.where(att[:, s : s + 1] == e, prod, qacc[s])
+            return carry
+
+        lax.fori_loop(0, experts, step, 0)
+        if h + 2 < heads:
+            fetch_q(h + 2).start()
+        for s in range(topk):
+            qall[h][0, s * suffix : (s + 1) * suffix, :] = rope(qacc[s]).astype(BF16)
+
+    def project_keys():
+        fetch_k.wait()
+        keys = jnp.dot(normed[...], kvbuf[0], preferred_element_type=F32)
+        for h in range(heads):
+            k_in[h] = rope(keys[:, h * HD : (h + 1) * HD]).astype(BF16)
+
+    def project_values():
+        fetch_v.wait()
+        vals = jnp.dot(normed[...], kvbuf[1], preferred_element_type=F32)
+        for h in range(heads):
+            vt_in[h] = vals[:, h * HD : (h + 1) * HD].T.astype(BF16)
+
+    def route():
+        logits = jnp.dot(normed[...], router[...], preferred_element_type=F32)
+        lane = lax.broadcasted_iota(jnp.int32, logits.shape, 1)
+        picks = [
+            jnp.sum(jnp.where(lane == att[:, s : s + 1], logits, 0.0), axis=1, keepdims=True)
+            for s in range(topk)
+        ]
+        top = functools.reduce(jnp.maximum, picks)
+        raised = [jnp.exp(x - top) for x in picks]
+        total = functools.reduce(jnp.add, raised)
+        for s in range(topk):
+            gates[s * suffix : (s + 1) * suffix, :] = raised[s] / total
+
     pl.semaphore_wait(barrier, len(partners) + len(mates))
 
     def gather_copy(h, k):
@@ -183,19 +168,9 @@
             device_id_type=MESH,
         )
 
-    for h in range(heads):
-        local_q[h].wait()
-        gather_copy(h, 0).start()
-    for p in range(pages):
-        for h in range(heads):
-            vt[h, p] = vpool[p, :, h * HD : (h + 1) * HD].T
     ust[0] = jnp.zeros_like(ust[0])
     ustat[0, 0:1] = jnp.full((1, qrows), NEG, F32)
     ustat[0, 1:2] = jnp.zeros((1, qrows), F32)
-    for k in range(1, rounds):
-        for h in range(heads):
-            gather_copy(h, k - 1).wait_recv()
-            gather_copy(h, k).start()
 
     def scores_t(keys, queries):
         return (
@@ -262,53 +237,80 @@
             rstat[h][k][i, 0:1], rstat[h][k][i, 1:2], rbuf[h][k][i].astype(F32),
         )
 
-    for h in range(heads):
-        gather_copy(h, rounds - 1).wait_recv()
-        attend(h)
-        for c in reduce_copies(h, 0):
-            c.start()
-
     slot = lax.broadcasted_iota(jnp.int32, (suffix, qrows), 1) % suffix
     key_at = lax.broadcasted_iota(jnp.int32, (suffix, qrows), 0)
     mask = (key_at <= slot) & (key_at < length[0])
 
-    for k in range(rounds - 1):
+    def pass_on(h, k):
         n = 2 ** (rounds - 2 - k)
-        for h in range(heads):
-            for c in reduce_copies(h, k):
-                c.wait_recv()
-
-            def give(i, carry, h=h, k=k, n=n):
-                m, l, o = merge_at(h, k, n + i)
-                sstat[h][k + 1][i, 0:1] = m
-                sstat[h][k + 1][i, 1:2] = l
-                sbuf[h][k + 1][i] = o.astype(BF16)
-                return carry
-
-            lax.fori_loop(0, n, give, 0)
-            for c in reduce_copies(h, k + 1):
+        for c in reduce_copies(h, k):
+            c.wait_recv()
+
+        def give(i, carry, h=h, k=k, n=n):
+            m, l, o = merge_at(h, k, n + i)
+            sstat[h][k + 1][i, 0:1] = m
+            sstat[h][k + 1][i, 1:2] = l
+            sbuf[h][k + 1][i] = o.astype(BF16)
+            return carry
+
+        lax.fori_loop(0, n, give, 0)
+        for c in reduce_copies(h, k + 1):
+            c.start()
+
+        def keep(i, carry, h=h, k=k):
+            m, l, o = merge_at(h, k, i)
+            cstat[h, i, 0:1] = m
+            cstat[h, i, 1:2] = l
+            cur[h, i] = o
+            return carry
+
+        lax.fori_loop(0, n, keep, 0)
+        if k == 0:
+            s = jnp.where(mask, scores_t(k_in[h], qall[h][0]), NEG)
+            m_s = jnp.max(s, axis=0, keepdims=True)
+            w = jnp.exp(s - m_s)
+            l_s = jnp.sum(w, axis=0, keepdims=True)
+            o_s_ = jnp.dot(vt_in[h], w.astype(BF16), preferred_element_type=F32)
+            m, l, o = merged(
+                cstat[h, 0, 0:1], cstat[h, 0, 1:2], cur[h, 0], m_s, l_s, o_s_
+            )
+            cstat[h, 0, 0:1] = m
+            cstat[h, 0, 1:2] = l
+            cur[h, 0] = o
+
+
+    for t in range(heads + 2 * rounds - 1):
+        for k in range(rounds, -1, -1):
+            h = t - k
+            if 0 <= h < heads:
+                if k > 0:
+                    gather_copy(h, k - 1).wait_recv()
+                if k < rounds:
+                    if k == 0:
+                        project(h)
+                    gather_copy(h, k).start()
+        if t == 0:
+            fetch_k.start()
+            fetch_v.start()
+        if t == 1:
+            project_keys()
+        if t == 2:
+            project_values()
+            route()
+        if t == max(heads - 1, 2):
+            for c in loads:
                 c.start()
-
-            def keep(i, carry, h=h, k=k):
-                m, l, o = merge_at(h, k, i)
-                cstat[h, i, 0:1] = m
-                cstat[h, i, 1:2] = l
-                cur[h, i] = o
-                return carry
-
-            lax.fori_loop(0, n, keep, 0)
-            if k == 0:
-                s = jnp.where(mask, scores_t(k_in[h], q_in[h]), NEG)
-                m_s = jnp.max(s, axis=0, keepdims=True)
-                w = jnp.exp(s - m_s)
-                l_s = jnp.sum(w, axis=0, keepdims=True)
-                o_s_ = jnp.dot(vt_in[h], w.astype(BF16), preferred_element_type=F32)
-                m, l, o = merged(
-                    cstat[h, 0, 0:1], cstat[h, 0, 1:2], cur[h, 0], m_s, l_s, o_s_
-                )
-                cstat[h, 0, 0:1] = m
-                cstat[h, 0, 1:2] = l
-                cur[h, 0] = o
+        if t < heads:
+            for p in range(pages):
+                vt[t, p] = vpool[p, :, t * HD : (t + 1) * HD].T
+        for k in range(rounds - 2, -1, -1):
+            h = t - rounds - 1 - k
+            if 0 <= h < heads:
+                pass_on(h, k)
+        if 0 <= t - rounds < heads:
+            attend(t - rounds)
+            for c in reduce_copies(t - rounds, 0):
+                c.start()
 
     row = lax.broadcasted_iota(jnp.int32, (qrows, 1), 0) % suffix
     factor = gates[...] * (row < length[0]).astype(F32)
@@ -436,30 +438,6 @@
     vm = pl.BlockSpec(memory_space=pltpu.VMEM)
     sm = pl.BlockSpec(memory_space=pltpu.SMEM)
     hbm = pl.BlockSpec(memory_space=pl.ANY)
-    q, k, vt, gates = pl.pallas_call(
-        project_kernel,
-        out_shape=(
-            jax.ShapeDtypeStruct((heads, qrows, HD), BF16),
-            jax.ShapeDtypeStruct((heads, rows, HD), BF16),
-            jax.ShapeDtypeStruct((heads, HD, rows), BF16),
-            jax.ShapeDtypeStruct((qrows, 1), F32),
-        ),
-        in_specs=[vm] * 6 + [hbm] * 3,
-        out_specs=(vm,) * 4,
-        scratch_shapes=[
-            pltpu.VMEM((NBUF, model, cols), BF16),
-            pltpu.VMEM((2, model, cols), BF16),
-            pltpu.VMEM((rows, model), BF16),
-            pltpu.VMEM((topk, rows, cols), F32),
-            pltpu.SemaphoreType.DMA((NBUF,)),
-            pltpu.SemaphoreType.DMA((2,)),
-        ],
-        compiler_params=pltpu.CompilerParams(vmem_limit_bytes=40 * 2**20),
-        name="project",
-    )(
-        hidden, norm_gain.reshape(1, -1), w_router, att_experts,
-        jnp.asarray(cos), jnp.asarray(sin), w_query, w_key, w_value,
-    )
     sizes = [2 ** (rounds - 1 - k_) for k_ in range(rounds)]
     width = model // heads_dev
     dma = pltpu.SemaphoreType.DMA
@@ -485,21 +463,29 @@
             dma((heads, rounds)), dma((heads, rounds)),
             dma((heads, rounds)), dma((heads, rounds)),
             dma((levels,)), dma((levels,)),
-            dma((heads_dev,)), dma((heads,)),
+            dma((heads_dev,)), dma((2,)), dma((2,)),
+            pltpu.VMEM((2, experts, model, HD), BF16),
+            pltpu.VMEM((2, model, cols), BF16),
+            pltpu.VMEM((rows, model), BF16),
+            pltpu.VMEM((topk, rows, HD), F32),
+            pltpu.VMEM((heads, rows, HD), BF16),
+            pltpu.VMEM((heads, HD, rows), BF16),
+            pltpu.VMEM((qrows, 1), F32),
         ]
     )
     return pl.pallas_call(
         functools.partial(attend_kernel, tok_bits, head_bits, units),
         out_shape=jax.ShapeDtypeStruct((rows, width), BF16),
-        in_specs=[sm, sm] + [vm] * 7 + [hbm],
+        in_specs=[sm, sm] + [vm] * 8 + [hbm] * 4,
         out_specs=vm,
         scratch_shapes=scratch,
         compiler_params=pltpu.CompilerParams(
             collective_id=0, has_side_effects=True, vmem_limit_bytes=56 * 2**20
         ),
-        name="attend",
+        name="layer",
     )(
-        meta, suffix_len, q, k, vt, gates, att_experts, key_pool, value_pool,
+        meta, suffix_len, hidden, norm_gain.reshape(1, -1), w_router, att_experts,
+        jnp.asarray(cos), jnp.asarray(sin), key_pool, value_pool, w_query, w_key, w_value,
         w_out.reshape(experts * cols, model),
     )
 

time: 116 us -> 110 us (0.948)
  local copies, waits for them, and re-layouts: 13.8 us -> 5.85 us
    pallas_call x1, Pallas kernels: 90.1 us -> 99.1 us  [per_device(): pl.pallas_call(functools.partial(attend_kernel, tok_bits, head_bits, unit...]
    unnamed x25 -> x3, local copies, waits for them, and re-layouts: 12.6 us -> 4.74 us
    pallas_call x1 -> x0, Pallas kernels: 7.87 us -> none  [per_device(): pl.pallas_call(project_kernel, out_shape=(jax.ShapeDtypeStruct((heads, qr...]
where the time goes in v2:
time: 110 us; the launch traced here: 109 us
  Pallas kernels  99.1 us (90%)
  local copies, waits for them, and re-layouts  5.85 us (5%)
  other arithmetic  2.83 us (3%)
    pallas_call x1, Pallas kernels, per_device(): pl.pallas_call(functools.partial(attend_kernel, tok_bits, head_bits, unit...  99.1 us
    unnamed x3, local copies, waits for them, and re-layouts  4.74 us

profile of v2, /device:TPU:0, one launch (start us, length us, event | category | flops | bytes accessed | tf_op | source)
XLA Modules:
  0.0 108.5 jit_solution(3366816349602913278)
XLA Ops:
  0.7 0.7 broadcast_xor_fusion
  1.3 0.8 select_reduce_fusion.2
  2.2 0.8 eq.62
  2.9 0.2 select_reduce_fusion.1
  3.1 0.2 fusion
  3.3 0.1 compare_convert_fusion
  3.4 0.1 reshape.157
  3.5 0.1 select_reduce_fusion
  3.6 0.1 convert_reduce_fusion
  3.7 0.1 compare_convert_fusion.1
  3.8 0.1 reshape.154
  3.9 0.2 slice_reduce_fusion
  4.1 0.6 pad_add_fusion.meta
  4.6 1.4 %copy.22.att = s32[128,2]{1,0:T(8,128)} copy(s32[128,2]{0,1:T(2,128)} %param.28) | data formatting | bytes 2048 | tf_op args[12]
  6.1 1.8 %copy.21.router = bf16[2048,8]{1,0:T(8,128)(2,1)} copy(bf16[2048,8]{0,1:T(8,128)(2,1)} %param.18) | data formatting | bytes 65536 | tf_op args[2]
  7.8 99.1 %layer.1 = bf16[128,512]{1,0:T(8,128)(2,1)} custom-call(s32[4,16]{1,0:T(4,128)} %pad_add_fusion.meta, s32[1]{0:T(128)S(6)} %copy.24.length, bf16[128,2048]{1,0:T(8,128)(2,1)} %hidden.1, f32[1,2048]{1,0:T(1,128)} %bitcast.24, bf16[2048,8]{1,0:T(8,128)(2,1)} %copy.21.router, s32[128,2]{1,0:T(8,128)} %copy.22.att, f32[128,128]{1,0:T(8,128)} %constant.61.clone.cos, ...), custom_call_target="tpu_custom_call" | custom-call | tf_op jit(solution)/shard_map/layer/pallas_call | solution.py:476
  107.0 1.6 %copy.25 = bf16[128,512]{1,0:T(8,128)(2,1)} copy(bf16[128,512]{1,0:T(8,128)(2,1)} %layer.1) | data formatting | bytes 262144
  (7 shorter events, 0.0 us)

commit v3 on v2

--- a/solution.py
+++ b/solution.py
@@ -195,7 +195,7 @@
             )
             return carry
 
-        lax.fori_loop(0, units, unit, 0)
+        lax.fori_loop(0, units, unit, 0, unroll=4)
 
         def keep(i, carry):
             cur[h, i] = ust[meta[3, i]]
@@ -303,14 +303,14 @@
         if t < heads:
             for p in range(pages):
                 vt[t, p] = vpool[p, :, t * HD : (t + 1) * HD].T
+        if 0 <= t - rounds < heads:
+            attend(t - rounds)
+            for c in reduce_copies(t - rounds, 0):
+                c.start()
         for k in range(rounds - 2, -1, -1):
             h = t - rounds - 1 - k
             if 0 <= h < heads:
                 pass_on(h, k)
-        if 0 <= t - rounds < heads:
-            attend(t - rounds)
-            for c in reduce_copies(t - rounds, 0):
-                c.start()
 
     row = lax.broadcasted_iota(jnp.int32, (qrows, 1), 0) % suffix
     factor = gates[...] * (row < length[0]).astype(F32)

time: 110 us -> 99.5 us (0.905); the launches traced: 109 us -> 99.2 us
  Pallas kernels: 99.1 us -> 89.8 us
    pallas_call x1, Pallas kernels: 99.1 us -> 89.8 us  [per_device(): pl.pallas_call(functools.partial(attend_kernel, tok_bits, head_bits, unit...]
where the time goes in v3:
time: 99.5 us; the launch traced here: 99.2 us
  Pallas kernels  89.8 us (90%)
  local copies, waits for them, and re-layouts  5.85 us (6%)
  other arithmetic  2.83 us (3%)
    pallas_call x1, Pallas kernels, per_device(): pl.pallas_call(functools.partial(attend_kernel, tok_bits, head_bits, unit...  89.8 us
    unnamed x3, local copies, waits for them, and re-layouts  4.74 us

profile of v3, /device:TPU:0, one launch (start us, length us, event | category | flops | bytes accessed | tf_op | source)
XLA Modules:
  0.0 99.2 jit_solution(15801702504536643498)
XLA Ops:
  0.7 0.7 broadcast_xor_fusion
  1.3 0.8 select_reduce_fusion.2
  2.2 0.8 eq.62
  2.9 0.2 select_reduce_fusion.1
  3.1 0.2 fusion
  3.3 0.1 compare_convert_fusion
  3.4 0.1 reshape.157
  3.5 0.1 select_reduce_fusion
  3.6 0.1 convert_reduce_fusion
  3.7 0.1 compare_convert_fusion.1
  3.8 0.1 reshape.154
  3.9 0.2 slice_reduce_fusion
  4.1 0.6 pad_add_fusion.meta
  4.6 1.4 %copy.22.att = s32[128,2]{1,0:T(8,128)} copy(s32[128,2]{0,1:T(2,128)} %param.28) | data formatting | bytes 2048 | tf_op args[12]
  6.1 1.8 %copy.21.router = bf16[2048,8]{1,0:T(8,128)(2,1)} copy(bf16[2048,8]{0,1:T(8,128)(2,1)} %param.18) | data formatting | bytes 65536 | tf_op args[2]
  7.8 89.8 %layer.1 = bf16[128,512]{1,0:T(8,128)(2,1)} custom-call(s32[4,16]{1,0:T(4,128)} %pad_add_fusion.meta, s32[1]{0:T(128)S(6)} %copy.24.length, bf16[128,2048]{1,0:T(8,128)(2,1)} %hidden.1, f32[1,2048]{1,0:T(1,128)} %bitcast.24, bf16[2048,8]{1,0:T(8,128)(2,1)} %copy.21.router, s32[128,2]{1,0:T(8,128)} %copy.22.att, f32[128,128]{1,0:T(8,128)} %constant.61.clone.cos, ...), custom_call_target="tpu_custom_call" | custom-call | tf_op jit(solution)/shard_map/layer/pallas_call | solution.py:476
  97.7 1.6 %copy.25 = bf16[128,512]{1,0:T(8,128)(2,1)} copy(bf16[128,512]{1,0:T(8,128)(2,1)} %layer.1) | data formatting | bytes 262144
  (7 shorter events, 0.0 us)

commit v4 on v3

--- a/solution.py
+++ b/solution.py
@@ -195,7 +195,7 @@
             )
             return carry
 
-        lax.fori_loop(0, units, unit, 0, unroll=4)
+        lax.fori_loop(0, units, unit, 0, unroll=True)
 
         def keep(i, carry):
             cur[h, i] = ust[meta[3, i]]

time: 99.5 us -> 98.1 us (0.986)
  Pallas kernels: 89.8 us -> 88.4 us
    pallas_call x1, Pallas kernels: 89.8 us -> 88.4 us  [per_device(): pl.pallas_call(functools.partial(attend_kernel, tok_bits, head_bits, unit...]
where the time goes in v4:
time: 98.1 us; the launch traced here: 97.8 us
  Pallas kernels  88.4 us (90%)
  local copies, waits for them, and re-layouts  5.85 us (6%)
  other arithmetic  2.83 us (3%)
    pallas_call x1, Pallas kernels, per_device(): pl.pallas_call(functools.partial(attend_kernel, tok_bits, head_bits, unit...  88.4 us
    unnamed x3, local copies, waits for them, and re-layouts  4.74 us

profile of v4, /device:TPU:0, one launch (start us, length us, event | category | flops | bytes accessed | tf_op | source)
XLA Modules:
  0.0 97.8 jit_solution(10887597104967293848)
XLA Ops:
  0.7 0.7 broadcast_xor_fusion
  1.3 0.8 select_reduce_fusion.2
  2.2 0.8 eq.62
  2.9 0.2 select_reduce_fusion.1
  3.1 0.2 fusion
  3.3 0.1 compare_convert_fusion
  3.4 0.1 reshape.157
  3.5 0.1 select_reduce_fusion
  3.6 0.1 convert_reduce_fusion
  3.7 0.1 compare_convert_fusion.1
  3.8 0.1 reshape.154
  3.9 0.2 slice_reduce_fusion
  4.1 0.6 pad_add_fusion.meta
  4.6 1.4 %copy.22.att = s32[128,2]{1,0:T(8,128)} copy(s32[128,2]{0,1:T(2,128)} %param.28) | data formatting | bytes 2048 | tf_op args[12]
  6.1 1.8 %copy.21.router = bf16[2048,8]{1,0:T(8,128)(2,1)} copy(bf16[2048,8]{0,1:T(8,128)(2,1)} %param.18) | data formatting | bytes 65536 | tf_op args[2]
  7.8 88.4 %layer.1 = bf16[128,512]{1,0:T(8,128)(2,1)} custom-call(s32[4,16]{1,0:T(4,128)} %pad_add_fusion.meta, s32[1]{0:T(128)S(6)} %copy.24.length, bf16[128,2048]{1,0:T(8,128)(2,1)} %hidden.1, f32[1,2048]{1,0:T(1,128)} %bitcast.24, bf16[2048,8]{1,0:T(8,128)(2,1)} %copy.21.router, s32[128,2]{1,0:T(8,128)} %copy.22.att, f32[128,128]{1,0:T(8,128)} %constant.61.clone.cos, ...), custom_call_target="tpu_custom_call" | custom-call | tf_op jit(solution)/shard_map/layer/pallas_call | solution.py:476
  96.2 1.6 %copy.25 = bf16[128,512]{1,0:T(8,128)(2,1)} copy(bf16[128,512]{1,0:T(8,128)(2,1)} %layer.1) | data formatting | bytes 262144
  (7 shorter events, 0.0 us)
